TPU v7x, 32 devices: a whole 2x2x4 slice. The times are simulated.
32 devices in a mesh: gx: 8 (over y, x, core), gy: 4 (over z).
Axes of the slice: x: 2, y: 2, z: 4, core: 2. Of those that a mesh axis runs over, the one named last changes fastest.
Arguments:
- e_field: float32 [3, 128, 32, 256], P(None, 'gx', 'gy'), may hold values from -6 to 6
- h_field: float32 [3, 128, 32, 256], P(None, 'gx', 'gy'), may hold values from -6 to 6
- currents: float32 [3, 128, 32, 256], P(None, 'gx', 'gy'), may hold values from -6 to 6
- material: int32 [128, 32, 256], P('gx', 'gy'), may hold values from 0 to 3
- coating: int32 [128, 32, 256], P('gx', 'gy'), may hold values 0 or 1
- mat_ca: float32 [4], replicated, may hold values from 0.4 to 1
- mat_cb: float32 [4], replicated, may hold values from 0.3 to 0.6
- drude: float32 [2], replicated, may hold values from 0.3 to 0.9
- inc_ez: float32 [4, 128], replicated, may hold values from -6 to 6
- inc_hy: float32 [4, 128], replicated, may hold values from -6 to 6
- box: int32 [6], replicated, may hold values from 1 to 254, as said below
Outputs:
- e_out: float32 [3, 128, 32, 256], P(None, 'gx', 'gy')
- h_out: float32 [3, 128, 32, 256], P(None, 'gx', 'gy')
- j_out: float32 [3, 128, 32, 256], P(None, 'gx', 'gy')
Inputs may be any that keep to these rules, and one draw needn't show every extreme that they name: `box`: 1 <= x0 < 32 and 96 <= x1 <= 126; 1 <= y0 < 8 and 24 <= y1 <= 30; 1 <= z0 < 64 and 192 <= z1 <= 254; some lower bound is 1, and the upper bound along the longest dimension is that dimension's cells minus 2.
All inputs are finite; a program needn't handle non-finite values. No bound on the sum of `coating` on one device may be relied on, other than what follows from the above.
Results may differ from a plain program's by a relative error of at most 0.0001.
Values sent between devices are 32-bit elements; how exact they have to be, the bound alone decides.
A program may use at most 64 MiB of HBM per device.

v0:
```python
import jax
import jax.numpy as jnp
from jax import lax
from jax.sharding import PartitionSpec as P

STEPS = 4
NMAT = 4


CH = 0.5


def passed_along(block, axis, distance):
    devices = range(lax.axis_size(axis))
    route = [(i - distance, i) for i in devices if i - distance in devices]
    return lax.ppermute(block, axis, route)


def flag(cond):
    return cond.astype(jnp.float32)


def lookup(line, where_at):
    return jnp.sum(jnp.where(jnp.arange(line.shape[0], dtype=jnp.int32) == where_at, line, 0.0))


def h_sources(line, box, xi, yi, zi, local):
    wx = flag((xi >= box[0]) & (xi <= box[1]))
    wy = flag((yi >= box[2]) & (yi <= box[3]))
    wz = flag((zi >= box[4]) & (zi <= box[5]))
    fx = flag(xi == box[0] - 1) * -lookup(line, box[0]) + flag(xi == box[1]) * lookup(line, box[1])
    dhy = CH * fx[:, None, None] * wy[None, :, None] * wz[None, None, :]
    fy = flag(yi == box[2] - 1) - flag(yi == box[3])
    dhx = CH * (local * wx)[:, None, None] * fy[None, :, None] * wz[None, None, :]
    return (dhx, dhy)


def e_sources(line, box, xi, yi, zi, local):
    wy = flag((yi >= box[2]) & (yi <= box[3]))
    wz = flag((zi >= box[4]) & (zi <= box[5]))
    fx = flag(xi == box[0]) * -lookup(line, box[0] - 1) + flag(xi == box[1]) * lookup(line, box[1])
    dez = fx[:, None, None] * wy[None, :, None] * wz[None, None, :]
    wopen = flag((xi >= box[0]) & (xi < box[1]))
    fz = flag(zi == box[4]) - flag(zi == box[5])
    dex = (local * wopen)[:, None, None] * wy[None, :, None] * fz[None, None, :]
    return (dex, dez)


def zfwd(field):
    return jnp.concatenate([field[:, :, 1:], jnp.zeros_like(field[:, :, :1])], 2) - field


def zbwd(field):
    return field - jnp.concatenate([jnp.zeros_like(field[:, :, :1]), field[:, :, :-1]], 2)


def curl_e(e, up_x, up_y):
    ex, ey, ez = (e[0], e[1], e[2])
    dez_dx = jnp.concatenate([ez[1:], up_x[1]], 0) - ez
    dey_dx = jnp.concatenate([ey[1:], up_x[0]], 0) - ey
    dez_dy = jnp.concatenate([ez[:, 1:], up_y[1]], 1) - ez
    dex_dy = jnp.concatenate([ex[:, 1:], up_y[0]], 1) - ex
    return (zfwd(ey) - dez_dy, dez_dx - zfwd(ex), dex_dy - dey_dx)


def curl_h(h, low_x, low_y):
    hx, hy, hz = (h[0], h[1], h[2])
    dhz_dy = hz - jnp.concatenate([low_y[1], hz[:, :-1]], 1)
    dhx_dy = hx - jnp.concatenate([low_y[0], hx[:, :-1]], 1)
    dhz_dx = hz - jnp.concatenate([low_x[1], hz[:-1]], 0)
    dhy_dx = hy - jnp.concatenate([low_x[0], hy[:-1]], 0)
    return (dhz_dy - zbwd(hy), zbwd(hx) - dhz_dx, dhy_dx - dhx_dy)


def e_rims(efield):
    send_x = efield[:, :1]
    send_y = efield[:, :, :1]
    got_x = passed_along(send_x, "gx", -1)
    got_y = passed_along(send_y, "gy", -1)
    return (got_x[1:3], got_y[0::2])


def h_rims(hfield):
    send_x = hfield[:, -1:]
    send_y = hfield[:, :, -1:]
    got_x = passed_along(send_x, "gx", 1)
    got_y = passed_along(send_y, "gy", 1)
    return (got_x[1:3], got_y[0::2])


def body(e_field, h_field, currents, material, coating, mat_ca, mat_cb, drude, inc_ez, inc_hy, box):
    ca = jnp.zeros(material.shape, jnp.float32)
    cb = jnp.zeros(material.shape, jnp.float32)
    for index in range(NMAT):
        ca = ca + flag(material == index) * mat_ca[index]
        cb = cb + flag(material == index) * mat_cb[index]
    coat = flag(coating == 1)
    width_x, width_y, depth = material.shape
    start_x = lax.axis_index("gx") * width_x
    start_y = lax.axis_index("gy") * width_y
    xi = start_x + jnp.arange(width_x, dtype=jnp.int32)
    yi = start_y + jnp.arange(width_y, dtype=jnp.int32)
    zi = jnp.arange(depth, dtype=jnp.int32)
    efield, hfield, jfield = (e_field, h_field, currents)
    for step in range(STEPS):
        up_x, up_y = e_rims(efield)
        curl_x, curl_y, curl_z = curl_e(efield, up_x, up_y)
        local_e = lax.dynamic_slice_in_dim(inc_ez[step], start_x, width_x)
        dhx, dhy = h_sources(inc_ez[step], box, xi, yi, zi, local_e)
        hfield = jnp.stack(
            [hfield[0] + CH * curl_x + dhx, hfield[1] + CH * curl_y + dhy, hfield[2] + CH * curl_z]
        )
        jfield = coat[None] * (drude[0] * jfield + drude[1] * efield)
        low_x, low_y = h_rims(hfield)
        cur_x, cur_y, cur_z = curl_h(hfield, low_x, low_y)
        local_h = lax.dynamic_slice_in_dim(inc_hy[step], start_x, width_x)
        dex, dez = e_sources(inc_hy[step], box, xi, yi, zi, local_h)
        efield = jnp.stack(
            [
                ca * efield[0] + cb * (cur_x + dex - jfield[0]),
                ca * efield[1] + cb * (cur_y - jfield[1]),
                ca * efield[2] + cb * (cur_z + dez - jfield[2]),
            ]
        )
    return (efield, hfield, jfield)


def solution(mesh):
    return jax.shard_map(
        body,
        mesh=mesh,
        in_specs=(
            P(None, "gx", "gy", None),
            P(None, "gx", "gy", None),
            P(None, "gx", "gy", None),
            P("gx", "gy", None),
            P("gx", "gy", None),
            P(),
            P(),
            P(),
            P(),
            P(),
            P(),
        ),
        out_specs=(P(None, "gx", "gy", None), P(None, "gx", "gy", None), P(None, "gx", "gy", None)),
        check_vma=False,
    )
```

profile of v0, /device:TPU:4, one launch (start us, length us, event | category | flops | bytes accessed | tf_op | source)
XLA Modules:
  0.0 158.9 jit_solution(771293066874318644)
XLA Ops:
  0.6 1.1 slice.588
  1.7 1.3 collective-permute-start
  3.0 0.7 slice.593
  3.8 2.8 %collective-permute-start.1 = (f32[3,1,8,256]{3,2,1,0:T(8,128)S(1)}, f32[3,1,8,256]{3,2,1,0:T(8,128)S(1)}, u32[]{:S(2)}, u32[]{:S(2)}) collective-permute-start(f32[3,1,8,256]{3,2,1,0:T(8,128)S(1)} %slice.593), channel_id=1, source_target_pairs={{4,0},{8,4},{12,8},{16,12},{20,16},{24,20},{28,24},{5,1},{9,5},{13... | collective-permute-start | bytes 73736 | tf_op jit(solution)/shard_map/ppermute | solution.py:16
  6.6 1.0 slice_bitcast_fusion.47
  7.6 0.7 copy-done.12
  8.3 0.6 fusion.156
  8.9 0.7 copy-done.7
  9.6 0.7 fusion.155
  10.3 0.7 copy-done.9
  11.7 1.2 and_convert_fusion
  12.9 0.6 fusion.107
  14.2 2.0 %fusion.128 = (f32[]{:T(128)}, f32[]{:T(128)}, f32[]{:T(128)}, f32[]{:T(128)}, f32[]{:T(128)}, /*index=5*/f32[]{:T(128)}, f32[]{:T(128)}, f32[]{:T(128)}, f32[]{...) fusion(s32[]{:T(128)S(6)} %sub.308, ...), kind=kLoop, calls=%fused_computation.267 | loop fusion | flops 4464 | bytes 4172 | tf_op jit(solution)/shard_map/reduce_sum | solution.py:24
  21.3 0.7 fusion.154
  22.0 0.6 fusion.153
  22.6 1.3 and_convert_fusion.1
  23.9 2.0 %select_add_fusion.2 = (f32[16]{0:T(128)S(1)}, pred[16]{0:T(512)(128)(4,1)S(1)}, pred[16]{0:T(512)(128)(4,1)S(1)}) fusion(f32[]{:T(128)} %get-tuple-element.7, f32[]{:T(128)S(6)} %neg.31, s32[]{:T(128)} %bitcast.17, s32[]{:T(128)S(6)} %mul.870, s32[]{:T(128)} %bitcast.18), kind=kLoop, calls=%fused_computation.297 | loop fusion | flops 96 | bytes 116 | tf_op jit(solution)/shard_map/add | solution.py:41
  25.8 1.4 fusion.125
  27.2 1.4 add_multiply_fusion.3
  28.8 2.6 %select_add_fusion.3 = (f32[16]{0:T(128)S(1)}, f32[16]{0:T(128)S(1)}, f32[16]{0:T(128)S(1)}, f32[16]{0:T(128)S(1)}, pred[16]{0:T(512)(128)(4,1)S(1)}) fusion(pred[16]{0:T(512)(128)(4,1)S(1)} %get-tuple-element.23, pred[16]{0:T(512)(128)(4,1)S(1)} %get-tuple-element.22, f32[]{:T(128)} %get-tuple-element.6, f32[]{:T(128)S(6)} %neg.29, f32[]{:T(128)} %get-tuple-element.5, ...), kind=kLoop, calls=%fused_computation.299 | loop fusion | flops 240 | bytes 344 | tf_op jit(solution)/shard_map/add | solution.py:41
  31.4 1.9 %add_multiply_fusion.5 = (f32[16]{0:T(128)S(1)}, f32[16]{0:T(128)S(1)}, f32[16]{0:T(128)S(1)}) fusion(pred[16]{0:T(512)(128)(4,1)S(1)} %get-tuple-element.23, pred[16]{0:T(512)(128)(4,1)S(1)} %get-tuple-element.126, f32[]{:T(128)} %get-tuple-element.152, f32[]{:T(128)S(6)} %neg.28, f32[]{:T(128)} %get-tuple-element.153, f32[]{:T(128)S(6)} %neg.26, ...), kind=kLoop, calls=%fused_computation.300 | loop fusion | flops 192 | bytes 248 | tf_op jit(solution)/shard_map/mul | solution.py:32
  33.3 0.1 broadcast_multiply_fusion.1
  33.4 1.3 fusion.106
  35.1 0.1 fusion.45
  35.3 1.9 %collective-permute-start.3 = (f32[3,1,8,256]{3,2,1,0:T(8,128)S(1)}, f32[3,1,8,256]{3,2,1,0:T(8,128)S(1)}, u32[]{:S(2)}, u32[]{:S(2)}) collective-permute-start(f32[3,1,8,256]{3,2,1,0:T(8,128)S(1)} %pad_maximum_fusion.12), channel_id=1, source_target_pairs={{0,4},{4,8},{8,12},{12,16},{16,20},{20,24},{24,28},{1,5},{5,9},{9,... | collective-permute-start | bytes 73736 | tf_op jit(solution)/shard_map/ppermute | solution.py:16
  37.2 4.3 %collective-permute-start.2 = (f32[3,16,1,256]{3,2,1,0:T(1,128)S(1)}, f32[3,16,1,256]{3,2,1,0:T(1,128)S(1)}, u32[]{:S(2)}, u32[]{:S(2)}) collective-permute-start(f32[3,16,1,256]{3,2,1,0:T(1,128)S(1)} %pad_maximum_fusion.7), channel_id=1, source_target_pairs={{0,1},{1,2},{2,3},{4,5},{5,6},{6,7},{8,9},{9,10},{10,11},{12,13},{... | collective-permute-start | bytes 147464 | tf_op jit(solution)/shard_map/ppermute | solution.py:16
  41.6 2.0 %collective-permute-done.2 = f32[3,16,1,256]{3,2,1,0:T(1,128)S(1)} collective-permute-done((f32[3,16,1,256]{3,2,1,0:T(1,128)S(1)}, f32[3,16,1,256]{3,2,1,0:T(1,128)S(1)}, u32[]{:S(2)}, u32[]{:S(2)}) %collective-permute-start.2) | collective-permute-done | bytes 49184 | tf_op jit(solution)/shard_map/ppermute | solution.py:16
  43.6 5.2 %fusion.38 = (f32[16,8,256]{2,1,0:T(8,128)S(1)}, pred[16,8,256]{2,1,0:T(8,128)(4,1)S(1)}, pred[16,8,256]{2,1,0:T(8,128)(4,1)S(1)}, pred[16,8,256]{2,1,0:T(8,128)(4,1)S(1)}, pred[16,8,256]{2,1,0:T(8,128)(4,1)S(1)}) fusion(f32[3,16,8,256]{3,2,1,0:T(8,128)S(1)} %add_multiply_fusion.3, f32[16,8,256]{2,1,0:T(8,128)S(1)} %fusion.41, ...), kind=kLoop, calls=%fused_computation.59 | loop fusion | flops 917504 | bytes 1180704 | tf_op jit(solution)/shard_map/add | solution.py:120
  48.7 5.1 %fusion.35 = f32[16,8,256]{2,1,0:T(8,128)S(1)} fusion(f32[3,16,8,256]{3,2,1,0:T(8,128)S(1)} %add_multiply_fusion.3, f32[16,8,256]{2,1,0:T(8,128)S(1)} %fusion.41, f32[15,8,256]{2,1,0:T(8,128)S(1)} %slice.740, f32[1,8,256]{2,1,0:T(8,128)S(1)} %get-tuple-element.87, f32[16,8,256]{2,1,0:T(8,128)S(1)} %get-tuple-element.33, f32[16,8,255]{2,1,0:T(8,128)S(1)} %bitcast.358, ...), kind=kLoop, calls=%fused_computation.55 | loop fusion | flops 720896 | bytes 1048096 | tf_op jit(solution)/shard_map/add | solution.py:121
  53.8 5.1 %fusion.32 = f32[16,8,256]{2,1,0:T(8,128)S(1)} fusion(f32[3,16,8,256]{3,2,1,0:T(8,128)S(1)} %add_multiply_fusion.3, f32[16,8,256]{2,1,0:T(8,128)S(1)} %get-tuple-element.34, f32[15,8,256]{2,1,0:T(8,128)S(1)} %slice.743, f32[1,8,256]{2,1,0:T(8,128)S(1)} %get-tuple-element.88, f32[16,8,256]{2,1,0:T(8,128)S(1)} %get-tuple-element.33, ...), kind=kLoop, calls=%fused_computation.51 | loop fusion | flops 819200 | bytes 1050144 | tf_op jit(solution)/shard_map/add | solution.py:122
  58.9 1.4 pad_maximum_fusion
  60.3 3.3 %collective-permute-start.5 = (f32[3,1,8,256]{3,2,1,0:T(8,128)S(1)}, f32[3,1,8,256]{3,2,1,0:T(8,128)S(1)}, u32[]{:S(2)}, u32[]{:S(2)}) collective-permute-start(f32[3,1,8,256]{3,2,1,0:T(8,128)S(1)} %slice.750), channel_id=1, source_target_pairs={{4,0},{8,4},{12,8},{16,12},{20,16},{24,20},{28,24},{5,1},{9,5},{13... | collective-permute-start | bytes 73736 | tf_op jit(solution)/shard_map/ppermute | solution.py:16
  64.0 1.3 collective-permute-start.4
  65.3 4.7 %collective-permute-done.4 = f32[3,16,1,256]{3,2,1,0:T(1,128)S(1)} collective-permute-done((f32[3,16,1,256]{3,2,1,0:T(1,128)S(1)}, f32[3,16,1,256]{3,2,1,0:T(1,128)S(1)}, u32[]{:S(2)}, u32[]{:S(2)}) %collective-permute-start.4) | collective-permute-done | bytes 49184 | tf_op jit(solution)/shard_map/ppermute | solution.py:16
  70.0 0.1 fusion.64
  70.2 1.9 %collective-permute-start.7 = (f32[3,1,8,256]{3,2,1,0:T(8,128)S(1)}, f32[3,1,8,256]{3,2,1,0:T(8,128)S(1)}, u32[]{:S(2)}, u32[]{:S(2)}) collective-permute-start(f32[3,1,8,256]{3,2,1,0:T(8,128)S(1)} %pad_maximum_fusion.10), channel_id=1, source_target_pairs={{0,4},{4,8},{8,12},{12,16},{16,20},{20,24},{24,28},{1,5},{5,9},{9,... | collective-permute-start | bytes 73736 | tf_op jit(solution)/shard_map/ppermute | solution.py:16
  72.2 3.9 %collective-permute-start.6 = (f32[3,16,1,256]{3,2,1,0:T(1,128)S(1)}, f32[3,16,1,256]{3,2,1,0:T(1,128)S(1)}, u32[]{:S(2)}, u32[]{:S(2)}) collective-permute-start(f32[3,16,1,256]{3,2,1,0:T(1,128)S(1)} %pad_maximum_fusion.6), channel_id=1, source_target_pairs={{0,1},{1,2},{2,3},{4,5},{5,6},{6,7},{8,9},{9,10},{10,11},{12,13},{... | collective-permute-start | bytes 147464 | tf_op jit(solution)/shard_map/ppermute | solution.py:16
  76.1 0.1 collective-permute-done.7
  76.2 5.1 %fusion.26 = f32[16,8,256]{2,1,0:T(8,128)S(1)} fusion(f32[3,16,8,256]{3,2,1,0:T(8,128)S(1)} %get-tuple-element.40, f32[16,8,256]{2,1,0:T(8,128)S(1)} %get-tuple-element.55, f32[15,8,256]{2,1,0:T(8,128)S(1)} %slice.765, f32[1,8,256]{2,1,0:T(8,128)S(1)} %get-tuple-element.83, f32[16,8,256]{2,1,0:T(8,128)S(1)} %get-tuple-element.53, ...), kind=kLoop, calls=%fused_computation.43 | loop fusion | flops 720896 | bytes 1048096 | tf_op jit(solution)/shard_map/add | solution.py:121
  81.3 5.1 %fusion.29 = f32[16,8,256]{2,1,0:T(8,128)S(1)} fusion(f32[3,16,8,256]{3,2,1,0:T(8,128)S(1)} %get-tuple-element.40, f32[16,8,256]{2,1,0:T(8,128)S(1)} %get-tuple-element.55, f32[16,7,256]{2,1,0:T(8,128)S(1)} %bitcast.379, f32[16,1,256]{2,1,0:T(1,128)S(1)} %get-tuple-element.66, f32[16,8,256]{2,1,0:T(8,128)S(1)} %get-tuple-element.54, ...), kind=kLoop, calls=%fused_computation.47 | loop fusion | flops 786432 | bytes 1049632 | tf_op jit(solution)/shard_map/add | solution.py:120
  86.5 5.1 %fusion.23 = f32[16,8,256]{2,1,0:T(8,128)S(1)} fusion(f32[3,16,8,256]{3,2,1,0:T(8,128)S(1)} %get-tuple-element.40, f32[16,8,256]{2,1,0:T(8,128)S(1)} %get-tuple-element.54, f32[15,8,256]{2,1,0:T(8,128)S(1)} %slice.768, f32[1,8,256]{2,1,0:T(8,128)S(1)} %get-tuple-element.84, f32[16,8,256]{2,1,0:T(8,128)S(1)} %get-tuple-element.53, ...), kind=kLoop, calls=%fused_computation.39 | loop fusion | flops 819200 | bytes 1050144 | tf_op jit(solution)/shard_map/add | solution.py:122
  91.6 1.4 pad_maximum_fusion.1
  93.0 4.2 %collective-permute-start.9 = (f32[3,1,8,256]{3,2,1,0:T(8,128)S(1)}, f32[3,1,8,256]{3,2,1,0:T(8,128)S(1)}, u32[]{:S(2)}, u32[]{:S(2)}) collective-permute-start(f32[3,1,8,256]{3,2,1,0:T(8,128)S(1)} %slice.775), channel_id=1, source_target_pairs={{4,0},{8,4},{12,8},{16,12},{20,16},{24,20},{28,24},{5,1},{9,5},{13... | collective-permute-start | bytes 73736 | tf_op jit(solution)/shard_map/ppermute | solution.py:16
  97.5 1.3 collective-permute-start.8
  98.8 4.7 %collective-permute-done.8 = f32[3,16,1,256]{3,2,1,0:T(1,128)S(1)} collective-permute-done((f32[3,16,1,256]{3,2,1,0:T(1,128)S(1)}, f32[3,16,1,256]{3,2,1,0:T(1,128)S(1)}, u32[]{:S(2)}, u32[]{:S(2)}) %collective-permute-start.8) | collective-permute-done | bytes 49184 | tf_op jit(solution)/shard_map/ppermute | solution.py:16
  103.5 0.1 fusion.80
  103.6 1.9 %collective-permute-start.11 = (f32[3,1,8,256]{3,2,1,0:T(8,128)S(1)}, f32[3,1,8,256]{3,2,1,0:T(8,128)S(1)}, u32[]{:S(2)}, u32[]{:S(2)}) collective-permute-start(f32[3,1,8,256]{3,2,1,0:T(8,128)S(1)} %pad_maximum_fusion.8), channel_id=1, source_target_pairs={{0,4},{4,8},{8,12},{12,16},{16,20},{20,24},{24,28},{1,5},{5,9},{9,... | collective-permute-start | bytes 73736 | tf_op jit(solution)/shard_map/ppermute | solution.py:16
  105.6 3.5 %collective-permute-start.10 = (f32[3,16,1,256]{3,2,1,0:T(1,128)S(1)}, f32[3,16,1,256]{3,2,1,0:T(1,128)S(1)}, u32[]{:S(2)}, u32[]{:S(2)}) collective-permute-start(f32[3,16,1,256]{3,2,1,0:T(1,128)S(1)} %pad_maximum_fusion.5), channel_id=1, source_target_pairs={{0,1},{1,2},{2,3},{4,5},{5,6},{6,7},{8,9},{9,10},{10,11},{12,13},{... | collective-permute-start | bytes 147464 | tf_op jit(solution)/shard_map/ppermute | solution.py:16
  109.1 0.5 collective-permute-done.11
  109.7 5.1 %fusion.17 = f32[16,8,256]{2,1,0:T(8,128)S(1)} fusion(f32[3,16,8,256]{3,2,1,0:T(8,128)S(1)} %get-tuple-element.38, f32[16,8,256]{2,1,0:T(8,128)S(1)} %get-tuple-element.52, f32[15,8,256]{2,1,0:T(8,128)S(1)} %slice.790, f32[1,8,256]{2,1,0:T(8,128)S(1)} %get-tuple-element.79, f32[16,8,256]{2,1,0:T(8,128)S(1)} %get-tuple-element.50, ...), kind=kLoop, calls=%fused_computation.31 | loop fusion | flops 720896 | bytes 1048096 | tf_op jit(solution)/shard_map/add | solution.py:121
  114.8 5.1 %fusion.20 = f32[16,8,256]{2,1,0:T(8,128)S(1)} fusion(f32[3,16,8,256]{3,2,1,0:T(8,128)S(1)} %get-tuple-element.38, f32[16,8,256]{2,1,0:T(8,128)S(1)} %get-tuple-element.52, f32[16,7,256]{2,1,0:T(8,128)S(1)} %bitcast.376, f32[16,1,256]{2,1,0:T(1,128)S(1)} %get-tuple-element.62, f32[16,8,256]{2,1,0:T(8,128)S(1)} %get-tuple-element.51, ...), kind=kLoop, calls=%fused_computation.35 | loop fusion | flops 786432 | bytes 1049632 | tf_op jit(solution)/shard_map/add | solution.py:120
  119.9 5.1 %fusion.14 = f32[16,8,256]{2,1,0:T(8,128)S(1)} fusion(f32[3,16,8,256]{3,2,1,0:T(8,128)S(1)} %get-tuple-element.38, f32[16,8,256]{2,1,0:T(8,128)S(1)} %get-tuple-element.51, f32[15,8,256]{2,1,0:T(8,128)S(1)} %slice.793, f32[1,8,256]{2,1,0:T(8,128)S(1)} %get-tuple-element.80, f32[16,8,256]{2,1,0:T(8,128)S(1)} %get-tuple-element.50, ...), kind=kLoop, calls=%fused_computation.27 | loop fusion | flops 819200 | bytes 1050144 | tf_op jit(solution)/shard_map/add | solution.py:122
  125.0 1.4 pad_maximum_fusion.2
  126.4 3.7 %collective-permute-start.13 = (f32[3,1,8,256]{3,2,1,0:T(8,128)S(1)}, f32[3,1,8,256]{3,2,1,0:T(8,128)S(1)}, u32[]{:S(2)}, u32[]{:S(2)}) collective-permute-start(f32[3,1,8,256]{3,2,1,0:T(8,128)S(1)} %slice.800), channel_id=1, source_target_pairs={{4,0},{8,4},{12,8},{16,12},{20,16},{24,20},{28,24},{5,1},{9,5},{13... | collective-permute-start | bytes 73736 | tf_op jit(solution)/shard_map/ppermute | solution.py:16
  130.5 1.3 collective-permute-start.12
  131.8 4.7 %collective-permute-done.12 = f32[3,16,1,256]{3,2,1,0:T(1,128)S(1)} collective-permute-done((f32[3,16,1,256]{3,2,1,0:T(1,128)S(1)}, f32[3,16,1,256]{3,2,1,0:T(1,128)S(1)}, u32[]{:S(2)}, u32[]{:S(2)}) %collective-permute-start.12) | collective-permute-done | bytes 49184 | tf_op jit(solution)/shard_map/ppermute | solution.py:16
  136.5 0.2 fusion.96
  136.7 1.9 %collective-permute-start.15 = (f32[3,1,8,256]{3,2,1,0:T(8,128)S(1)}, f32[3,1,8,256]{3,2,1,0:T(8,128)S(1)}, u32[]{:S(2)}, u32[]{:S(2)}) collective-permute-start(f32[3,1,8,256]{3,2,1,0:T(8,128)S(1)} %slice.814), channel_id=1, source_target_pairs={{0,4},{4,8},{8,12},{12,16},{16,20},{20,24},{24,28},{1,5},{5,9},{9,... | collective-permute-start | bytes 73736 | tf_op jit(solution)/shard_map/ppermute | solution.py:16
  138.7 2.2 %collective-permute-start.14 = (f32[3,16,1,256]{3,2,1,0:T(1,128)S(1)}, f32[3,16,1,256]{3,2,1,0:T(1,128)S(1)}, u32[]{:S(2)}, u32[]{:S(2)}) collective-permute-start(f32[3,16,1,256]{3,2,1,0:T(1,128)S(1)} %slice.808), channel_id=1, source_target_pairs={{0,1},{1,2},{2,3},{4,5},{5,6},{6,7},{8,9},{9,10},{10,11},{12,13},{... | collective-permute-start | bytes 147464 | tf_op jit(solution)/shard_map/ppermute | solution.py:16
  140.9 1.8 %collective-permute-done.15 = f32[3,1,8,256]{3,2,1,0:T(8,128)S(1)} collective-permute-done((f32[3,1,8,256]{3,2,1,0:T(8,128)S(1)}, f32[3,1,8,256]{3,2,1,0:T(8,128)S(1)}, u32[]{:S(2)}, u32[]{:S(2)}) %collective-permute-start.15) | collective-permute-done | bytes 24608 | tf_op jit(solution)/shard_map/ppermute | solution.py:16
  142.8 5.1 %fusion.7 = f32[1,16,8,256]{3,2,1,0:T(8,128)S(1)} fusion(f32[3,16,8,256]{3,2,1,0:T(8,128)S(1)} %get-tuple-element.36, f32[16,8,256]{2,1,0:T(8,128)S(1)} %get-tuple-element.49, f32[15,8,256]{2,1,0:T(8,128)S(1)} %slice.816, f32[1,8,256]{2,1,0:T(8,128)S(1)} %get-tuple-element.75, f32[16,8,256]{2,1,0:T(8,128)S(1)} %get-tuple-element.47, ...), kind=kLoop, calls=%fused_computation.18 | loop fusion | flops 720896 | bytes 1048096 | tf_op jit(solution)/shard_map/stack | solution.py:118
  147.9 5.1 %fusion.11 = f32[1,16,8,256]{3,2,1,0:T(8,128)S(1)} fusion(f32[3,16,8,256]{3,2,1,0:T(8,128)S(1)} %get-tuple-element.36, f32[16,8,256]{2,1,0:T(8,128)S(1)} %get-tuple-element.49, f32[16,7,256]{2,1,0:T(8,128)S(1)} %bitcast.395, f32[16,1,256]{2,1,0:T(1,128)S(1)} %get-tuple-element.58, f32[16,8,256]{2,1,0:T(8,128)S(1)} %get-tuple-element.48, ...), kind=kLoop, calls=%fused_computation.23 | loop fusion | flops 786432 | bytes 1049632 | tf_op jit(solution)/shard_map/stack | solution.py:118
  153.0 5.1 %fusion.3 = f32[1,16,8,256]{3,2,1,0:T(8,128)S(1)} fusion(f32[3,16,8,256]{3,2,1,0:T(8,128)S(1)} %get-tuple-element.36, f32[16,8,256]{2,1,0:T(8,128)S(1)} %get-tuple-element.48, f32[15,8,256]{2,1,0:T(8,128)S(1)} %slice.819, f32[1,8,256]{2,1,0:T(8,128)S(1)} %get-tuple-element.76, f32[16,8,256]{2,1,0:T(8,128)S(1)} %get-tuple-element.47, ...), kind=kLoop, calls=%fused_computation.13 | loop fusion | flops 819200 | bytes 1050144 | tf_op jit(solution)/shard_map/stack | solution.py:118
  158.2 0.8 pad_maximum_fusion.4
  (110 shorter events, 2.0 us)
Async XLA Ops:
  0.6 6.9 %copy-start = (f32[3,16,8,256]{3,2,1,0:T(8,128)S(1)}, f32[3,16,8,256]{3,2,1,0:T(8,128)}, u32[]{:S(2)}) copy-start(f32[3,16,8,256]{3,2,1,0:T(8,128)} %param.11) | copy-start | bytes 1179652
  1.7 33.1 %collective-permute-start = (f32[3,16,1,256]{3,2,1,0:T(1,128)S(1)}, f32[3,16,1,256]{3,2,1,0:T(1,128)S(1)}, u32[]{:S(2)}, u32[]{:S(2)}) collective-permute-start(f32[3,16,1,256]{3,2,1,0:T(1,128)S(1)} %slice.588), channel_id=1, source_target_pairs={{1,0},{2,1},{3,2},{5,4},{6,5},{7,6},{9,8},{10,9},{11,10},{13,12},{... | collective-permute-start | bytes 147464 | tf_op jit(solution)/shard_map/ppermute | solution.py:16
  3.8 31.0 %collective-permute-start.1 = (f32[3,1,8,256]{3,2,1,0:T(8,128)S(1)}, f32[3,1,8,256]{3,2,1,0:T(8,128)S(1)}, u32[]{:S(2)}, u32[]{:S(2)}) collective-permute-start(f32[3,1,8,256]{3,2,1,0:T(8,128)S(1)} %slice.593), channel_id=1, source_target_pairs={{4,0},{8,4},{12,8},{16,12},{20,16},{24,20},{28,24},{5,1},{9,5},{13... | collective-permute-start | bytes 73736 | tf_op jit(solution)/shard_map/ppermute | solution.py:16
  7.6 1.3 copy-start.5
  7.6 0.7 copy-start.12
  8.9 18.4 %copy-start.4 = (f32[3,16,8,256]{3,2,1,0:T(8,128)S(1)}, f32[3,16,8,256]{3,2,1,0:T(8,128)}, u32[]{:S(2)}) copy-start(f32[3,16,8,256]{3,2,1,0:T(8,128)} %param.13) | copy-start | bytes 1179652
  8.9 0.7 copy-start.7
  9.6 0.7 copy-start.8
  10.3 0.7 copy-start.9
  18.7 3.2 %copy-start.11 = (f32[4]{0:T(128)S(1)}, f32[4]{0:T(128)}, u32[]{:S(2)}) copy-start(f32[4]{0:T(128)} %param.17) | copy-start | bytes 52
  20.6 0.7 copy-start.10
  28.6 6.3 %copy-start.2 = (f32[3,16,8,256]{3,2,1,0:T(8,128)S(1)}, f32[3,16,8,256]{3,2,1,0:T(8,128)}, u32[]{:S(2)}) copy-start(f32[3,16,8,256]{3,2,1,0:T(8,128)} %param.12) | copy-start | bytes 1179652
  35.3 6.3 %collective-permute-start.3 = (f32[3,1,8,256]{3,2,1,0:T(8,128)S(1)}, f32[3,1,8,256]{3,2,1,0:T(8,128)S(1)}, u32[]{:S(2)}, u32[]{:S(2)}) collective-permute-start(f32[3,1,8,256]{3,2,1,0:T(8,128)S(1)} %pad_maximum_fusion.12), channel_id=1, source_target_pairs={{0,4},{4,8},{8,12},{12,16},{16,20},{20,24},{24,28},{1,5},{5,9},{9,... | collective-permute-start | bytes 73736 | tf_op jit(solution)/shard_map/ppermute | solution.py:16
  37.2 6.3 %collective-permute-start.2 = (f32[3,16,1,256]{3,2,1,0:T(1,128)S(1)}, f32[3,16,1,256]{3,2,1,0:T(1,128)S(1)}, u32[]{:S(2)}, u32[]{:S(2)}) collective-permute-start(f32[3,16,1,256]{3,2,1,0:T(1,128)S(1)} %pad_maximum_fusion.7), channel_id=1, source_target_pairs={{0,1},{1,2},{2,3},{4,5},{5,6},{6,7},{8,9},{9,10},{10,11},{12,13},{... | collective-permute-start | bytes 147464 | tf_op jit(solution)/shard_map/ppermute | solution.py:16
  41.5 2.0 %copy-start.6 = (s32[16,8,256]{2,1,0:T(8,128)S(1)}, s32[16,8,256]{2,1,0:T(8,128)}, u32[]{:S(2)}) copy-start(s32[16,8,256]{2,1,0:T(8,128)} %param.14) | copy-start | bytes 393220
  60.3 5.0 %collective-permute-start.5 = (f32[3,1,8,256]{3,2,1,0:T(8,128)S(1)}, f32[3,1,8,256]{3,2,1,0:T(8,128)S(1)}, u32[]{:S(2)}, u32[]{:S(2)}) collective-permute-start(f32[3,1,8,256]{3,2,1,0:T(8,128)S(1)} %slice.750), channel_id=1, source_target_pairs={{4,0},{8,4},{12,8},{16,12},{20,16},{24,20},{28,24},{5,1},{9,5},{13... | collective-permute-start | bytes 73736 | tf_op jit(solution)/shard_map/ppermute | solution.py:16
  64.0 6.0 %collective-permute-start.4 = (f32[3,16,1,256]{3,2,1,0:T(1,128)S(1)}, f32[3,16,1,256]{3,2,1,0:T(1,128)S(1)}, u32[]{:S(2)}, u32[]{:S(2)}) collective-permute-start(f32[3,16,1,256]{3,2,1,0:T(1,128)S(1)} %slice.747), channel_id=1, source_target_pairs={{1,0},{2,1},{3,2},{5,4},{6,5},{7,6},{9,8},{10,9},{11,10},{13,12},{... | collective-permute-start | bytes 147464 | tf_op jit(solution)/shard_map/ppermute | solution.py:16
  70.2 6.0 %collective-permute-start.7 = (f32[3,1,8,256]{3,2,1,0:T(8,128)S(1)}, f32[3,1,8,256]{3,2,1,0:T(8,128)S(1)}, u32[]{:S(2)}, u32[]{:S(2)}) collective-permute-start(f32[3,1,8,256]{3,2,1,0:T(8,128)S(1)} %pad_maximum_fusion.10), channel_id=1, source_target_pairs={{0,4},{4,8},{8,12},{12,16},{16,20},{20,24},{24,28},{1,5},{5,9},{9,... | collective-permute-start | bytes 73736 | tf_op jit(solution)/shard_map/ppermute | solution.py:16
  72.2 9.1 %collective-permute-start.6 = (f32[3,16,1,256]{3,2,1,0:T(1,128)S(1)}, f32[3,16,1,256]{3,2,1,0:T(1,128)S(1)}, u32[]{:S(2)}, u32[]{:S(2)}) collective-permute-start(f32[3,16,1,256]{3,2,1,0:T(1,128)S(1)} %pad_maximum_fusion.6), channel_id=1, source_target_pairs={{0,1},{1,2},{2,3},{4,5},{5,6},{6,7},{8,9},{9,10},{10,11},{12,13},{... | collective-permute-start | bytes 147464 | tf_op jit(solution)/shard_map/ppermute | solution.py:16
  93.0 5.8 %collective-permute-start.9 = (f32[3,1,8,256]{3,2,1,0:T(8,128)S(1)}, f32[3,1,8,256]{3,2,1,0:T(8,128)S(1)}, u32[]{:S(2)}, u32[]{:S(2)}) collective-permute-start(f32[3,1,8,256]{3,2,1,0:T(8,128)S(1)} %slice.775), channel_id=1, source_target_pairs={{4,0},{8,4},{12,8},{16,12},{20,16},{24,20},{28,24},{5,1},{9,5},{13... | collective-permute-start | bytes 73736 | tf_op jit(solution)/shard_map/ppermute | solution.py:16
  97.5 6.0 %collective-permute-start.8 = (f32[3,16,1,256]{3,2,1,0:T(1,128)S(1)}, f32[3,16,1,256]{3,2,1,0:T(1,128)S(1)}, u32[]{:S(2)}, u32[]{:S(2)}) collective-permute-start(f32[3,16,1,256]{3,2,1,0:T(1,128)S(1)} %slice.772), channel_id=1, source_target_pairs={{1,0},{2,1},{3,2},{5,4},{6,5},{7,6},{9,8},{10,9},{11,10},{13,12},{... | collective-permute-start | bytes 147464 | tf_op jit(solution)/shard_map/ppermute | solution.py:16
  103.6 6.0 %collective-permute-start.11 = (f32[3,1,8,256]{3,2,1,0:T(8,128)S(1)}, f32[3,1,8,256]{3,2,1,0:T(8,128)S(1)}, u32[]{:S(2)}, u32[]{:S(2)}) collective-permute-start(f32[3,1,8,256]{3,2,1,0:T(8,128)S(1)} %pad_maximum_fusion.8), channel_id=1, source_target_pairs={{0,4},{4,8},{8,12},{12,16},{16,20},{20,24},{24,28},{1,5},{5,9},{9,... | collective-permute-start | bytes 73736 | tf_op jit(solution)/shard_map/ppermute | solution.py:16
  105.6 9.1 %collective-permute-start.10 = (f32[3,16,1,256]{3,2,1,0:T(1,128)S(1)}, f32[3,16,1,256]{3,2,1,0:T(1,128)S(1)}, u32[]{:S(2)}, u32[]{:S(2)}) collective-permute-start(f32[3,16,1,256]{3,2,1,0:T(1,128)S(1)} %pad_maximum_fusion.5), channel_id=1, source_target_pairs={{0,1},{1,2},{2,3},{4,5},{5,6},{6,7},{8,9},{9,10},{10,11},{12,13},{... | collective-permute-start | bytes 147464 | tf_op jit(solution)/shard_map/ppermute | solution.py:16
  126.4 26.6 %copy-start.1 = (f32[3,16,8,256]{3,2,1,0:T(8,128)}, f32[3,16,8,256]{3,2,1,0:T(8,128)S(1)}, u32[]{:S(2)}) copy-start(f32[3,16,8,256]{3,2,1,0:T(8,128)S(1)} %get-tuple-element.36) | copy-start | bytes 1179652
  126.4 5.4 %collective-permute-start.13 = (f32[3,1,8,256]{3,2,1,0:T(8,128)S(1)}, f32[3,1,8,256]{3,2,1,0:T(8,128)S(1)}, u32[]{:S(2)}, u32[]{:S(2)}) collective-permute-start(f32[3,1,8,256]{3,2,1,0:T(8,128)S(1)} %slice.800), channel_id=1, source_target_pairs={{4,0},{8,4},{12,8},{16,12},{20,16},{24,20},{28,24},{5,1},{9,5},{13... | collective-permute-start | bytes 73736 | tf_op jit(solution)/shard_map/ppermute | solution.py:16
  130.5 6.0 %collective-permute-start.12 = (f32[3,16,1,256]{3,2,1,0:T(1,128)S(1)}, f32[3,16,1,256]{3,2,1,0:T(1,128)S(1)}, u32[]{:S(2)}, u32[]{:S(2)}) collective-permute-start(f32[3,16,1,256]{3,2,1,0:T(1,128)S(1)} %slice.797), channel_id=1, source_target_pairs={{1,0},{2,1},{3,2},{5,4},{6,5},{7,6},{9,8},{10,9},{11,10},{13,12},{... | collective-permute-start | bytes 147464 | tf_op jit(solution)/shard_map/ppermute | solution.py:16
  136.7 11.2 %copy-start.3 = (f32[3,16,8,256]{3,2,1,0:T(8,128)}, f32[3,16,8,256]{3,2,1,0:T(8,128)S(1)}, u32[]{:S(2)}) copy-start(f32[3,16,8,256]{3,2,1,0:T(8,128)S(1)} %pad_maximum_fusion.3) | copy-start | bytes 1179652
  136.7 6.0 %collective-permute-start.15 = (f32[3,1,8,256]{3,2,1,0:T(8,128)S(1)}, f32[3,1,8,256]{3,2,1,0:T(8,128)S(1)}, u32[]{:S(2)}, u32[]{:S(2)}) collective-permute-start(f32[3,1,8,256]{3,2,1,0:T(8,128)S(1)} %slice.814), channel_id=1, source_target_pairs={{0,4},{4,8},{8,12},{12,16},{16,20},{20,24},{24,28},{1,5},{5,9},{9,... | collective-permute-start | bytes 73736 | tf_op jit(solution)/shard_map/ppermute | solution.py:16
  138.7 9.1 %collective-permute-start.14 = (f32[3,16,1,256]{3,2,1,0:T(1,128)S(1)}, f32[3,16,1,256]{3,2,1,0:T(1,128)S(1)}, u32[]{:S(2)}, u32[]{:S(2)}) collective-permute-start(f32[3,16,1,256]{3,2,1,0:T(1,128)S(1)} %slice.808), channel_id=1, source_target_pairs={{0,1},{1,2},{2,3},{4,5},{5,6},{6,7},{8,9},{9,10},{10,11},{12,13},{... | collective-permute-start | bytes 147464 | tf_op jit(solution)/shard_map/ppermute | solution.py:16
where the time goes:
time: 161 us; the launch traced here: 159 us
  other arithmetic  82.9 us (51%)
  starting transfers between devices  40.8 us (25%)
  waiting for transfers between devices  18.4 us (11%)
  local copies, waits for them, and re-layouts  8.79 us (5%)
  between operations  7.99 us (5%)
    ppermute x16, starting transfers between devices, passed_along(): return lax.ppermute(block, axis, route)  40.8 us
    another operation x7, other arithmetic, body(): jnp.stack([ca * efield[0] + cb * (cur_x + dex - jfield[0]), ca * efield[1...  20.2 us
    ppermute x16, waiting for transfers between devices, passed_along(): return lax.ppermute(block, axis, route)  18.4 us
    add x3, other arithmetic, body(): ca * efield[0] + cb * (cur_x + dex - jfield[0])  15.4 us
    add x3, other arithmetic, body(): ca * efield[2] + cb * (cur_z + dez - jfield[2])  15.3 us
    add x3, other arithmetic, body(): ca * efield[1] + cb * (cur_y - jfield[1])  15.3 us
    add x2, other arithmetic, e_sources(): flag(xi == box[0]) * -lookup(line, box[0] - 1)  4.52 us
  transfers between devices with their start and end apart: 16, of which 7 were waited for; matrix products, arithmetic and copies ran while one was open for 23% of the time, Pallas kernels for 0%

commit v1 on v0

v1 whole, which is shorter than its diff:
```python
import functools

import jax
import jax.numpy as jnp
from jax import lax
from jax.experimental import pallas as pl
from jax.experimental.pallas import tpu as pltpu
from jax.sharding import PartitionSpec as P

CH = 0.5
MESH = pl.DeviceIdType.MESH

EX, EY, HX, HY, CEY, CEX = range(6)


def kernel(nx, ny, e_in, h_in, j_in, mat_in, coat_in, mat_ca, mat_cb, drude, inc_ez, inc_hy, box,
           e_out, h_out, j_out, E, H, J, M, C, CA, CB,
           s_ex, s_ey, s_hx, s_hy, s_cey, s_cex, r_ex, r_ey, r_hx, r_hy, r_cey, r_cex, low_y,
           load_sem, store_sem, send_sem, recv_sem):
    gx, gy = lax.axis_index("gx"), lax.axis_index("gy")
    steps = inc_ez.shape[0]
    wx, wy, depth = M.shape
    line_len = inc_ez.shape[1]

    loads = [pltpu.make_async_copy(src, dst, load_sem.at[i])
             for i, (src, dst) in enumerate([(mat_in, M), (coat_in, C), (e_in, E), (h_in, H), (j_in, J)])]
    for copy in loads:
        copy.start()

    has_lx, has_ux, has_ly, has_uy = gx > 0, gx < nx - 1, gy > 0, gy < ny - 1
    down_up, up_down = has_lx & has_uy, has_ux & has_ly
    to_lx, to_ux = (gx - 1, gy), (gx + 1, gy)
    to_ly, to_uy = (gx, gy - 1), (gx, gy + 1)
    to_du, to_ud = (gx - 1, gy + 1), (gx + 1, gy - 1)
    kinds = [
        (s_ex, r_ex, to_lx, has_lx, has_ux),
        (s_ey, r_ey, to_ly, has_ly, has_uy),
        (s_hx, r_hx, to_ux, has_ux, has_lx),
        (s_hy, r_hy, to_uy, has_uy, has_ly),
        (s_cey, r_cey, to_du, down_up, up_down),
        (s_cex, r_cex, to_ud, up_down, down_up),
    ]

    for _, dst, _, _, comes in kinds:
        @pl.when(jnp.logical_not(comes))
        def _():
            dst[...] = jnp.zeros_like(dst)

    barrier = pltpu.get_barrier_semaphore()
    for target, exists in [(to_lx, has_lx), (to_ux, has_ux), (to_ly, has_ly), (to_uy, has_uy),
                           (to_du, down_up), (to_ud, up_down)]:
        @pl.when(exists)
        def _():
            pl.semaphore_signal(barrier, inc=1, device_id=target, device_id_type=MESH)

    def copy_of(kind, step):
        src, dst, target, _, _ = kinds[kind]
        return pltpu.make_async_remote_copy(
            src_ref=src.at[step], dst_ref=dst.at[step], send_sem=send_sem.at[step, kind],
            recv_sem=recv_sem.at[step, kind], device_id=target, device_id_type=MESH)

    def send(kind, step):
        @pl.when(kinds[kind][3])
        def _():
            copy_of(kind, step).start()

    x0, x1, y0, y1, z0, z1 = [box[i] for i in range(6)]
    shape = (wy, depth)
    row = lax.broadcasted_iota(jnp.int32, shape, 0)
    lane = lax.broadcasted_iota(jnp.int32, shape, 1)
    yi = row + gy * wy
    first_row, last_row = row == 0, row == wy - 1
    first_lane, last_lane = lane == 0, lane == depth - 1
    in_y = (yi >= y0) & (yi <= y1)
    in_z = (lane >= z0) & (lane <= z1)
    f32 = lambda cond: jnp.where(cond, 1.0, 0.0).astype(jnp.float32)
    zero = jnp.zeros(shape, jnp.float32)
    w_yz = f32(in_y & in_z)
    fy_z = (f32(yi == y0 - 1) - f32(yi == y1)) * f32(in_z) * CH
    y_fz = f32(in_y) * (f32(lane == z0) - f32(lane == z1))
    start_x = gx * wx

    zup = lambda f: jnp.where(last_lane, zero, pltpu.roll(f, depth - 1, 1))
    zdn = lambda f: jnp.where(first_lane, zero, pltpu.roll(f, 1, 1))
    yup = lambda f: pltpu.roll(f, wy - 1, 0)
    ydn = lambda f: pltpu.roll(f, 1, 0)

    loads[0].wait()
    a = [mat_ca[i] for i in range(mat_ca.shape[0])]
    b = [mat_cb[i] for i in range(mat_cb.shape[0])]
    for x in range(wx):
        m = M[x]
        va, vb = jnp.full(shape, a[0], jnp.float32), jnp.full(shape, b[0], jnp.float32)
        for i in range(1, len(a)):
            va, vb = jnp.where(m == i, a[i], va), jnp.where(m == i, b[i], vb)
        CA[x], CB[x] = va, vb
    kd, bd = drude[0], drude[1]
    for copy in loads[1:]:
        copy.wait()
    pl.semaphore_wait(barrier, sum(jnp.where(c, 1, 0) for c in (has_lx, has_ux, has_ly, has_uy, down_up, up_down)))

    def one_step(step, carry):
        s_ex[step, 0], s_ex[step, 1] = E[1, 0], E[2, 0]
        send(EX, step)
        for x in range(wx):
            s_ey[step, 0, pl.ds(x, 1), :] = E[0, x, pl.ds(0, 1), :]
            s_ey[step, 1, pl.ds(x, 1), :] = E[2, x, pl.ds(0, 1), :]
        send(EY, step)
        s_cey[step] = E[1, 0, pl.ds(wy - 1, 1), :]
        send(CEY, step)
        s_cex[step] = E[0, wx - 1, pl.ds(0, 1), :]
        send(CEX, step)

        ez_x0, ez_x1 = inc_ez[step, x0], inc_ez[step, x1]
        for x in range(wx):
            xi = start_x + x
            ex, ey, ez = E[0, x], E[1, x], E[2, x]
            ey_up = E[1, x + 1] if x + 1 < wx else zero
            ez_up = E[2, x + 1] if x + 1 < wx else zero
            ez_y = jnp.where(last_row, zero, yup(ez))
            ex_y = jnp.where(last_row, zero, yup(ex))
            fx = CH * (jnp.where(xi == x1, ez_x1, 0.0) - jnp.where(xi == x0 - 1, ez_x0, 0.0))
            local = jnp.where((xi >= x0) & (xi <= x1), inc_ez[step, xi], 0.0)
            hx = H[0, x] + CH * ((zup(ey) - ey) - (ez_y - ez)) + local * fy_z
            hy = H[1, x] + CH * ((ez_up - ez) - (zup(ex) - ex)) + fx * w_yz
            hz = H[2, x] + CH * ((ex_y - ex) - (ey_up - ey))
            H[0, x], H[1, x], H[2, x] = hx, hy, hz
            s_hy[step, 0, pl.ds(x, 1), :] = hx[wy - 1:wy]
            s_hy[step, 1, pl.ds(x, 1), :] = hz[wy - 1:wy]
        send(HY, step)
        s_hx[step, 0], s_hx[step, 1] = H[1, wx - 1], H[2, wx - 1]
        send(HX, step)

        hy_x0, hy_x1 = inc_hy[step, jnp.maximum(x0 - 1, 0)], inc_hy[step, x1]
        for x in range(wx):
            xi = start_x + x
            fx = jnp.where(xi == x1, hy_x1, 0.0) - jnp.where(xi == x0, hy_x0, 0.0)
            local = jnp.where((xi >= x0) & (xi < x1), inc_hy[step, xi], 0.0)
            coat = C[x] == 1
            ca, cb = CA[x], CB[x]
            for c in range(3):
                e = E[c, x]
                j = jnp.where(coat, kd * J[c, x] + bd * e, zero)
                J[c, x] = j
                t = -j
                if c == 0:
                    t = local * y_fz - j
                if c == 2:
                    t = fx * w_yz - j
                E[c, x] = ca * e + cb * t

        @pl.when(step == steps - 1)
        def _():
            pltpu.make_async_copy(J, j_out, store_sem.at[2]).start()

        for kind in range(6):
            @pl.when(kinds[kind][4])
            def _():
                copy_of(kind, step).wait_recv()

        has_y = jnp.where(has_ly, 1.0, 0.0).astype(jnp.float32)
        has_x = jnp.where(has_lx, 1.0, 0.0).astype(jnp.float32)
        low_y[0] = has_y * (r_hy[step, 0] - CH * s_ey[step, 1])
        low_y[1] = has_y * (r_hy[step, 1] + CH * s_ey[step, 0])
        low_y[1, pl.ds(wx - 1, 1), :] = low_y[1, pl.ds(wx - 1, 1), :] - (CH * has_y) * r_cey[step]
        hy_low = has_x * (r_hx[step, 0] + CH * s_ex[step, 1])
        corner = jnp.where(last_row, jnp.broadcast_to(r_cex[step], shape), zero)
        hz_low = has_x * (r_hx[step, 1] - CH * (s_ex[step, 0] - corner))
        for x in range(wx):
            ez_up = jnp.broadcast_to(r_ey[step, 1, pl.ds(x, 1), :], shape)
            ex_up = jnp.broadcast_to(r_ey[step, 0, pl.ds(x, 1), :], shape)
            hx = H[0, x] - jnp.where(last_row, CH * ez_up, zero)
            hy = H[1, x]
            hz = H[2, x] + jnp.where(last_row, CH * ex_up, zero)
            if x == wx - 1:
                hy = hy + CH * r_ex[step, 1]
                hz = hz - CH * r_ex[step, 0]
                H[1, x] = hy
            H[0, x], H[2, x] = hx, hz
            cb = CB[x]
            hx_y = jnp.where(first_row, jnp.broadcast_to(low_y[0, pl.ds(x, 1), :], shape), ydn(hx))
            hz_y = jnp.where(first_row, jnp.broadcast_to(low_y[1, pl.ds(x, 1), :], shape), ydn(hz))
            E[0, x] = E[0, x] + cb * ((hz - hz_y) - (hy - zdn(hy)))
            E[1, x] = E[1, x] + cb * ((hx - zdn(hx)) - (hz - hz_low))
            E[2, x] = E[2, x] + cb * ((hy - hy_low) - (hx - hx_y))
            hy_low, hz_low = hy, hz

        for kind in range(6):
            @pl.when(kinds[kind][3])
            def _():
                copy_of(kind, step).wait_send()
        return carry

    lax.fori_loop(0, steps, one_step, 0)
    stores = [pltpu.make_async_copy(E, e_out, store_sem.at[0]), pltpu.make_async_copy(H, h_out, store_sem.at[1])]
    for copy in stores:
        copy.start()
    for copy in stores:
        copy.wait()
    pltpu.make_async_copy(J, j_out, store_sem.at[2]).wait()


def body(nx, ny, e_field, h_field, currents, material, coating, mat_ca, mat_cb, drude, inc_ez, inc_hy, box):
    _, wx, wy, depth = e_field.shape
    steps = inc_ez.shape[0]
    hbm, smem = pl.BlockSpec(memory_space=pl.ANY), pl.BlockSpec(memory_space=pltpu.SMEM)
    field = pltpu.VMEM((3, wx, wy, depth), jnp.float32)
    cell = pltpu.VMEM((wx, wy, depth), jnp.float32)
    cell_int = pltpu.VMEM((wx, wy, depth), jnp.int32)
    x_plane = pltpu.VMEM((steps, 2, wy, depth), jnp.float32)
    y_plane = pltpu.VMEM((steps, 2, wx, depth), jnp.float32)
    corner = pltpu.VMEM((steps, 1, depth), jnp.float32)
    messages = [x_plane, y_plane, x_plane, y_plane, corner, corner]
    return pl.pallas_call(
        functools.partial(kernel, nx, ny),
        out_shape=[jax.ShapeDtypeStruct(e_field.shape, jnp.float32)] * 3,
        in_specs=[hbm] * 5 + [smem] * 6,
        out_specs=[hbm] * 3,
        scratch_shapes=[field, field, field, cell_int, cell_int, cell, cell]
        + messages + messages + [pltpu.VMEM((2, wx, depth), jnp.float32)]
        + [pltpu.SemaphoreType.DMA((5,)), pltpu.SemaphoreType.DMA((3,)),
           pltpu.SemaphoreType.DMA((steps, 6)), pltpu.SemaphoreType.DMA((steps, 6))],
        compiler_params=pltpu.CompilerParams(collective_id=0, has_side_effects=True),
    )(e_field, h_field, currents, material, coating, mat_ca, mat_cb, drude, inc_ez, inc_hy, box)


def solution(mesh):
    field, cell = P(None, "gx", "gy", None), P("gx", "gy", None)
    return jax.shard_map(
        functools.partial(body, mesh.shape["gx"], mesh.shape["gy"]),
        mesh=mesh,
        in_specs=(field, field, field, cell, cell, P(), P(), P(), P(), P(), P()),
        out_specs=(field, field, field),
        check_vma=False,
    )
```

time: 161 us -> 23.6 us (0.15)
  the two profiles are of different devices: /device:TPU:4 before, /device:TPU:0 now
where the time goes in v1:
time: 23.6 us; the launch traced here: 23.3 us
  Pallas kernels  19 us (81%)
  local copies, waits for them, and re-layouts  3.7 us (16%)
  between operations  0.65 us (3%)
    pallas_call x1, Pallas kernels, body(): pl.pallas_call(functools.partial(kernel, nx, ny), out_shape=[jax.ShapeDty...  19 us
    unnamed x7, local copies, waits for them, and re-layouts  3.7 us

profile of v1, /device:TPU:0, one launch (start us, length us, event | category | flops | bytes accessed | tf_op | source)
XLA Modules:
  0.0 23.3 jit_solution(12014691964902171368)
XLA Ops:
  0.6 19.0 %shard_map.130 = (f32[3,16,8,256]{3,2,1,0:T(8,128)}, f32[3,16,8,256]{3,2,1,0:T(8,128)}, f32[3,16,8,256]{3,2,1,0:T(8,128)}) custom-call(f32[3,16,8,256]{3,2,1,0:T(8,128)} %e_in.1, f32[3,16,8,256]{3,2,1,0:T(8,128)} %h_in.1, f32[3,16,8,256]{3,2,1,0:T(8,128)} %j_in.1, s32[16,8,256]{2,1,0:T(8,128)} %mat_in.1, s32[16,8,256]{2,1,0:T(8,128)} %coat_in.1, f32[4]{0:T(128)} %mat_ca.1, ...), custom_call_target="tpu_custom_call" | custom-call | tf_op jit(solution)/shard_map/pallas_call | solution.py:214
  19.6 0.0 copy-start.1
  19.6 1.8 %copy.17 = f32[3,16,8,256]{3,2,1,0:T(8,128)} copy(f32[3,16,8,256]{3,2,1,0:T(8,128)} %get-tuple-element.6) | data formatting | bytes 786432
  21.4 0.0 copy-done.1
  21.5 0.0 copy-start
  21.5 0.7 %copy.18 = f32[3,16,8,256]{3,2,1,0:T(8,128)} copy(f32[3,16,8,256]{3,2,1,0:T(8,128)S(1)} %copy-done.1) | data formatting | bytes 786432
  22.2 0.4 %copy-done = f32[3,16,8,256]{3,2,1,0:T(8,128)S(1)} copy-done((f32[3,16,8,256]{3,2,1,0:T(8,128)S(1)}, f32[3,16,8,256]{3,2,1,0:T(8,128)}, u32[]{:S(2)}) %copy-start) | copy-done | bytes 393240
  22.6 0.7 %copy.19 = f32[3,16,8,256]{3,2,1,0:T(8,128)} copy(f32[3,16,8,256]{3,2,1,0:T(8,128)S(1)} %copy-done) | data formatting | bytes 786432
Async XLA Ops:
  19.6 1.8 %copy-start.1 = (f32[3,16,8,256]{3,2,1,0:T(8,128)S(1)}, f32[3,16,8,256]{3,2,1,0:T(8,128)}, u32[]{:S(2)}) copy-start(f32[3,16,8,256]{3,2,1,0:T(8,128)} %get-tuple-element.7) | copy-start | bytes 1179652
  21.5 1.1 %copy-start = (f32[3,16,8,256]{3,2,1,0:T(8,128)S(1)}, f32[3,16,8,256]{3,2,1,0:T(8,128)}, u32[]{:S(2)}) copy-start(f32[3,16,8,256]{3,2,1,0:T(8,128)} %get-tuple-element.8) | copy-start | bytes 1179652

commit v2 on v1

--- a/solution.py
+++ b/solution.py
@@ -13,17 +13,19 @@
 EX, EY, HX, HY, CEY, CEX = range(6)
 
 
-def kernel(nx, ny, e_in, h_in, j_in, mat_in, coat_in, mat_ca, mat_cb, drude, inc_ez, inc_hy, box,
-           e_out, h_out, j_out, E, H, J, M, C, CA, CB,
+def kernel(nx, ny, e_in, h_in, j_in, mat_in, coat_in, ca_in, cb_in, drude_in, ez_in, hy_in, box_in,
+           E, H, J, M, C, CA, CB, mat_ca, mat_cb, drude, inc_ez, inc_hy, box,
            s_ex, s_ey, s_hx, s_hy, s_cey, s_cex, r_ex, r_ey, r_hx, r_hy, r_cey, r_cex, low_y,
-           load_sem, store_sem, send_sem, recv_sem):
+           load_sem, send_sem, recv_sem):
     gx, gy = lax.axis_index("gx"), lax.axis_index("gy")
     steps = inc_ez.shape[0]
     wx, wy, depth = M.shape
     line_len = inc_ez.shape[1]
 
     loads = [pltpu.make_async_copy(src, dst, load_sem.at[i])
-             for i, (src, dst) in enumerate([(mat_in, M), (coat_in, C), (e_in, E), (h_in, H), (j_in, J)])]
+             for i, (src, dst) in enumerate([
+                 (ca_in, mat_ca), (cb_in, mat_cb), (drude_in, drude), (ez_in, inc_ez), (hy_in, inc_hy),
+                 (box_in, box), (mat_in, M), (coat_in, C), (e_in, E), (h_in, H), (j_in, J)])]
     for copy in loads:
         copy.start()
 
@@ -64,6 +66,8 @@
         def _():
             copy_of(kind, step).start()
 
+    for copy in loads[:7]:
+        copy.wait()
     x0, x1, y0, y1, z0, z1 = [box[i] for i in range(6)]
     shape = (wy, depth)
     row = lax.broadcasted_iota(jnp.int32, shape, 0)
@@ -85,7 +89,6 @@
     yup = lambda f: pltpu.roll(f, wy - 1, 0)
     ydn = lambda f: pltpu.roll(f, 1, 0)
 
-    loads[0].wait()
     a = [mat_ca[i] for i in range(mat_ca.shape[0])]
     b = [mat_cb[i] for i in range(mat_cb.shape[0])]
     for x in range(wx):
@@ -95,7 +98,7 @@
             va, vb = jnp.where(m == i, a[i], va), jnp.where(m == i, b[i], vb)
         CA[x], CB[x] = va, vb
     kd, bd = drude[0], drude[1]
-    for copy in loads[1:]:
+    for copy in loads[7:]:
         copy.wait()
     pl.semaphore_wait(barrier, sum(jnp.where(c, 1, 0) for c in (has_lx, has_ux, has_ly, has_uy, down_up, up_down)))
 
@@ -149,10 +152,6 @@
                     t = fx * w_yz - j
                 E[c, x] = ca * e + cb * t
 
-        @pl.when(step == steps - 1)
-        def _():
-            pltpu.make_async_copy(J, j_out, store_sem.at[2]).start()
-
         for kind in range(6):
             @pl.when(kinds[kind][4])
             def _():
@@ -192,36 +191,51 @@
         return carry
 
     lax.fori_loop(0, steps, one_step, 0)
-    stores = [pltpu.make_async_copy(E, e_out, store_sem.at[0]), pltpu.make_async_copy(H, h_out, store_sem.at[1])]
-    for copy in stores:
+
+
+def write_out(*refs):
+    *ends, sems = refs
+    count = len(ends) // 2
+    copies = [pltpu.make_async_copy(src, dst, sems.at[i])
+              for i, (src, dst) in enumerate(zip(ends[:count], ends[count:]))]
+    for copy in copies:
         copy.start()
-    for copy in stores:
+    for copy in copies:
         copy.wait()
-    pltpu.make_async_copy(J, j_out, store_sem.at[2]).wait()
 
 
 def body(nx, ny, e_field, h_field, currents, material, coating, mat_ca, mat_cb, drude, inc_ez, inc_hy, box):
     _, wx, wy, depth = e_field.shape
     steps = inc_ez.shape[0]
-    hbm, smem = pl.BlockSpec(memory_space=pl.ANY), pl.BlockSpec(memory_space=pltpu.SMEM)
-    field = pltpu.VMEM((3, wx, wy, depth), jnp.float32)
+    hbm = pl.BlockSpec(memory_space=pltpu.HBM)
+    vmem = pl.BlockSpec(memory_space=pltpu.VMEM)
     cell = pltpu.VMEM((wx, wy, depth), jnp.float32)
     cell_int = pltpu.VMEM((wx, wy, depth), jnp.int32)
     x_plane = pltpu.VMEM((steps, 2, wy, depth), jnp.float32)
     y_plane = pltpu.VMEM((steps, 2, wx, depth), jnp.float32)
     corner = pltpu.VMEM((steps, 1, depth), jnp.float32)
     messages = [x_plane, y_plane, x_plane, y_plane, corner, corner]
+    small = (mat_ca, mat_cb, drude, inc_ez, inc_hy, box)
+    fields = pl.pallas_call(
+        functools.partial(kernel, nx, ny),
+        out_shape=[pltpu.VMEM(e_field.shape, jnp.float32)] * 3,
+        in_specs=[hbm] * 11,
+        out_specs=[vmem] * 3,
+        scratch_shapes=[cell_int, cell_int, cell, cell] + [pltpu.SMEM(a.shape, a.dtype) for a in small]
+        + messages + messages + [pltpu.VMEM((2, wx, depth), jnp.float32)]
+        + [pltpu.SemaphoreType.DMA((11,)),
+           pltpu.SemaphoreType.DMA((steps, 6)), pltpu.SemaphoreType.DMA((steps, 6))],
+        compiler_params=pltpu.CompilerParams(
+            collective_id=0, has_side_effects=True, vmem_limit_bytes=int(60 * 2**20)),
+    )(e_field, h_field, currents, material, coating, *small)
     return pl.pallas_call(
-        functools.partial(kernel, nx, ny),
+        write_out,
         out_shape=[jax.ShapeDtypeStruct(e_field.shape, jnp.float32)] * 3,
-        in_specs=[hbm] * 5 + [smem] * 6,
+        in_specs=[vmem] * 3,
         out_specs=[hbm] * 3,
-        scratch_shapes=[field, field, field, cell_int, cell_int, cell, cell]
-        + messages + messages + [pltpu.VMEM((2, wx, depth), jnp.float32)]
-        + [pltpu.SemaphoreType.DMA((5,)), pltpu.SemaphoreType.DMA((3,)),
-           pltpu.SemaphoreType.DMA((steps, 6)), pltpu.SemaphoreType.DMA((steps, 6))],
-        compiler_params=pltpu.CompilerParams(collective_id=0, has_side_effects=True),
-    )(e_field, h_field, currents, material, coating, mat_ca, mat_cb, drude, inc_ez, inc_hy, box)
+        scratch_shapes=[pltpu.SemaphoreType.DMA((3,))],
+        compiler_params=pltpu.CompilerParams(vmem_limit_bytes=8 * 2**20),
+    )(*fields)
 
 
 def solution(mesh):

time: 23.6 us -> 19.2 us (0.81)
  local copies, waits for them, and re-layouts: 3.7 us -> 0 us
  Pallas kernels: 19 us -> 18.4 us
    unnamed x7 -> x0, local copies, waits for them, and re-layouts: 3.7 us -> none
    pallas_call x1 -> x2, Pallas kernels: 19 us -> 18.4 us  [the longest x1 17.4 us: body(): pl.pallas_call(functools.partial(kernel, nx, ny), out_shape=[pltpu.VMEM(e...]
where the time goes in v2:
time: 19.2 us; the launch traced here: 19 us
  Pallas kernels  18.4 us (96%)
  between operations  0.64 us (3%)
    pallas_call x1, Pallas kernels, body(): pl.pallas_call(functools.partial(kernel, nx, ny), out_shape=[pltpu.VMEM(e...  17.4 us
    pallas_call x1, Pallas kernels, body(): pl.pallas_call(write_out, out_shape=[jax.ShapeDtypeStruct(e_field.shape,...  1.03 us

profile of v2, /device:TPU:0, one launch (start us, length us, event | category | flops | bytes accessed | tf_op | source)
XLA Modules:
  0.0 19.0 jit_solution(2285481975265409378)
XLA Ops:
  0.6 17.4 %shard_map.130 = (f32[3,16,8,256]{3,2,1,0:T(8,128)S(1)}, f32[3,16,8,256]{3,2,1,0:T(8,128)S(1)}, f32[3,16,8,256]{3,2,1,0:T(8,128)S(1)}) custom-call(f32[3,16,8,256]{3,2,1,0:T(8,128)} %e_in.1, f32[3,16,8,256]{3,2,1,0:T(8,128)} %h_in.1, f32[3,16,8,256]{3,2,1,0:T(8,128)} %j_in.1, s32[16,8,256]{2,1,0:T(8,128)} %mat_in.1, s32[16,8,256]{2,1,0:T(8,128)} %coat_in.1, ...), custom_call_target="tpu_custom_call" | custom-call | tf_op jit(solution)/shard_map/pallas_call | solution.py:219
  18.0 1.0 %shard_map.131 = (f32[3,16,8,256]{3,2,1,0:T(8,128)}, f32[3,16,8,256]{3,2,1,0:T(8,128)}, f32[3,16,8,256]{3,2,1,0:T(8,128)}) custom-call(f32[3,16,8,256]{3,2,1,0:T(8,128)S(1)} %get-tuple-element.6.refs_0_, f32[3,16,8,256]{3,2,1,0:T(8,128)S(1)} %get-tuple-element.7.refs_1_, f32[3,16,8,256]{3,2,1,0:T(8,128)S(1)} %get-tuple-element.8.refs_2_), custom_call_target="tpu_custom_call" | custom-call | tf_op jit(solution)/shard_map/pallas_call | solution.py:231

commit v3 on v2

--- a/solution.py
+++ b/solution.py
@@ -21,13 +21,6 @@
     steps = inc_ez.shape[0]
     wx, wy, depth = M.shape
     line_len = inc_ez.shape[1]
-
-    loads = [pltpu.make_async_copy(src, dst, load_sem.at[i])
-             for i, (src, dst) in enumerate([
-                 (ca_in, mat_ca), (cb_in, mat_cb), (drude_in, drude), (ez_in, inc_ez), (hy_in, inc_hy),
-                 (box_in, box), (mat_in, M), (coat_in, C), (e_in, E), (h_in, H), (j_in, J)])]
-    for copy in loads:
-        copy.start()
 
     has_lx, has_ux, has_ly, has_uy = gx > 0, gx < nx - 1, gy > 0, gy < ny - 1
     down_up, up_down = has_lx & has_uy, has_ux & has_ly
@@ -43,17 +36,24 @@
         (s_cex, r_cex, to_ud, up_down, down_up),
     ]
 
-    for _, dst, _, _, comes in kinds:
-        @pl.when(jnp.logical_not(comes))
-        def _():
-            dst[...] = jnp.zeros_like(dst)
-
     barrier = pltpu.get_barrier_semaphore()
     for target, exists in [(to_lx, has_lx), (to_ux, has_ux), (to_ly, has_ly), (to_uy, has_uy),
                            (to_du, down_up), (to_ud, up_down)]:
         @pl.when(exists)
         def _():
             pl.semaphore_signal(barrier, inc=1, device_id=target, device_id_type=MESH)
+
+    loads = [pltpu.make_async_copy(src, dst, load_sem.at[i])
+             for i, (src, dst) in enumerate([
+                 (ca_in, mat_ca), (cb_in, mat_cb), (drude_in, drude), (ez_in, inc_ez), (hy_in, inc_hy),
+                 (box_in, box), (mat_in, M), (coat_in, C), (e_in, E), (h_in, H), (j_in, J)])]
+    for copy in loads:
+        copy.start()
+
+    for _, dst, _, _, comes in kinds:
+        @pl.when(jnp.logical_not(comes))
+        def _():
+            dst[...] = jnp.zeros_like(dst)
 
     def copy_of(kind, step):
         src, dst, target, _, _ = kinds[kind]
@@ -102,40 +102,52 @@
         copy.wait()
     pl.semaphore_wait(barrier, sum(jnp.where(c, 1, 0) for c in (has_lx, has_ux, has_ly, has_uy, down_up, up_down)))
 
+    def stage_rows(step, x, ex, ez):
+        s_ey[step, 0, pl.ds(x, 1), :] = ex[:1]
+        s_ey[step, 1, pl.ds(x, 1), :] = ez[:1]
+
+    for x in range(wx):
+        stage_rows(0, x, E[0, x], E[2, x])
+
     def one_step(step, carry):
-        s_ex[step, 0], s_ex[step, 1] = E[1, 0], E[2, 0]
-        send(EX, step)
-        for x in range(wx):
-            s_ey[step, 0, pl.ds(x, 1), :] = E[0, x, pl.ds(0, 1), :]
-            s_ey[step, 1, pl.ds(x, 1), :] = E[2, x, pl.ds(0, 1), :]
-        send(EY, step)
         s_cey[step] = E[1, 0, pl.ds(wy - 1, 1), :]
         send(CEY, step)
         s_cex[step] = E[0, wx - 1, pl.ds(0, 1), :]
         send(CEX, step)
+        send(EY, step)
+        s_ex[step, 0], s_ex[step, 1] = E[1, 0], E[2, 0]
+        send(EX, step)
 
         ez_x0, ez_x1 = inc_ez[step, x0], inc_ez[step, x1]
         for x in range(wx):
             xi = start_x + x
             ex, ey, ez = E[0, x], E[1, x], E[2, x]
             ey_up = E[1, x + 1] if x + 1 < wx else zero
-            ez_up = E[2, x + 1] if x + 1 < wx else zero
             ez_y = jnp.where(last_row, zero, yup(ez))
             ex_y = jnp.where(last_row, zero, yup(ex))
-            fx = CH * (jnp.where(xi == x1, ez_x1, 0.0) - jnp.where(xi == x0 - 1, ez_x0, 0.0))
             local = jnp.where((xi >= x0) & (xi <= x1), inc_ez[step, xi], 0.0)
             hx = H[0, x] + CH * ((zup(ey) - ey) - (ez_y - ez)) + local * fy_z
-            hy = H[1, x] + CH * ((ez_up - ez) - (zup(ex) - ex)) + fx * w_yz
             hz = H[2, x] + CH * ((ex_y - ex) - (ey_up - ey))
-            H[0, x], H[1, x], H[2, x] = hx, hy, hz
+            H[0, x], H[2, x] = hx, hz
             s_hy[step, 0, pl.ds(x, 1), :] = hx[wy - 1:wy]
             s_hy[step, 1, pl.ds(x, 1), :] = hz[wy - 1:wy]
         send(HY, step)
+
+        def update_hy(x):
+            xi = start_x + x
+            ex, ez = E[0, x], E[2, x]
+            ez_up = E[2, x + 1] if x + 1 < wx else zero
+            fx = CH * (jnp.where(xi == x1, ez_x1, 0.0) - jnp.where(xi == x0 - 1, ez_x0, 0.0))
+            H[1, x] = H[1, x] + CH * ((ez_up - ez) - (zup(ex) - ex)) + fx * w_yz
+
+        update_hy(wx - 1)
         s_hx[step, 0], s_hx[step, 1] = H[1, wx - 1], H[2, wx - 1]
         send(HX, step)
 
         hy_x0, hy_x1 = inc_hy[step, jnp.maximum(x0 - 1, 0)], inc_hy[step, x1]
         for x in range(wx):
+            if x < wx - 1:
+                update_hy(x)
             xi = start_x + x
             fx = jnp.where(xi == x1, hy_x1, 0.0) - jnp.where(xi == x0, hy_x0, 0.0)
             local = jnp.where((xi >= x0) & (xi < x1), inc_hy[step, xi], 0.0)
@@ -153,18 +165,23 @@
                 E[c, x] = ca * e + cb * t
 
         for kind in range(6):
-            @pl.when(kinds[kind][4])
+            @pl.when(kinds[kind][3])
             def _():
-                copy_of(kind, step).wait_recv()
+                copy_of(kind, step).wait_send()
+        def receive(*which):
+            for kind in which:
+                @pl.when(kinds[kind][4])
+                def _():
+                    copy_of(kind, step).wait_recv()
+
+        receive(EX, HX, EY, HY)
 
         has_y = jnp.where(has_ly, 1.0, 0.0).astype(jnp.float32)
         has_x = jnp.where(has_lx, 1.0, 0.0).astype(jnp.float32)
         low_y[0] = has_y * (r_hy[step, 0] - CH * s_ey[step, 1])
         low_y[1] = has_y * (r_hy[step, 1] + CH * s_ey[step, 0])
-        low_y[1, pl.ds(wx - 1, 1), :] = low_y[1, pl.ds(wx - 1, 1), :] - (CH * has_y) * r_cey[step]
         hy_low = has_x * (r_hx[step, 0] + CH * s_ex[step, 1])
-        corner = jnp.where(last_row, jnp.broadcast_to(r_cex[step], shape), zero)
-        hz_low = has_x * (r_hx[step, 1] - CH * (s_ex[step, 0] - corner))
+        hz_low = has_x * (r_hx[step, 1] - CH * s_ex[step, 0])
         for x in range(wx):
             ez_up = jnp.broadcast_to(r_ey[step, 1, pl.ds(x, 1), :], shape)
             ex_up = jnp.broadcast_to(r_ey[step, 0, pl.ds(x, 1), :], shape)
@@ -179,15 +196,20 @@
             cb = CB[x]
             hx_y = jnp.where(first_row, jnp.broadcast_to(low_y[0, pl.ds(x, 1), :], shape), ydn(hx))
             hz_y = jnp.where(first_row, jnp.broadcast_to(low_y[1, pl.ds(x, 1), :], shape), ydn(hz))
-            E[0, x] = E[0, x] + cb * ((hz - hz_y) - (hy - zdn(hy)))
+            ex = E[0, x] + cb * ((hz - hz_y) - (hy - zdn(hy)))
+            ez = E[2, x] + cb * ((hy - hy_low) - (hx - hx_y))
+            E[0, x], E[2, x] = ex, ez
             E[1, x] = E[1, x] + cb * ((hx - zdn(hx)) - (hz - hz_low))
-            E[2, x] = E[2, x] + cb * ((hy - hy_low) - (hx - hx_y))
+            stage_rows(step + 1, x, ex, ez)
             hy_low, hz_low = hy, hz
 
-        for kind in range(6):
-            @pl.when(kinds[kind][3])
-            def _():
-                copy_of(kind, step).wait_send()
+        receive(CEY, CEX)
+        top, end = pl.ds(0, 1), pl.ds(wy - 1, 1)
+        line = E[0, wx - 1, top, :] + CB[wx - 1, top, :] * ((CH * has_y) * r_cey[step])
+        E[0, wx - 1, top, :] = line
+        s_ey[step + 1, 0, pl.ds(wx - 1, 1), :] = line
+        E[1, 0, end, :] = E[1, 0, end, :] + CB[0, end, :] * ((CH * has_x) * r_cex[step])
+
         return carry
 
     lax.fori_loop(0, steps, one_step, 0)
@@ -215,6 +237,7 @@
     y_plane = pltpu.VMEM((steps, 2, wx, depth), jnp.float32)
     corner = pltpu.VMEM((steps, 1, depth), jnp.float32)
     messages = [x_plane, y_plane, x_plane, y_plane, corner, corner]
+    sent = [x_plane, pltpu.VMEM((steps + 1, 2, wx, depth), jnp.float32)] + messages[2:]
     small = (mat_ca, mat_cb, drude, inc_ez, inc_hy, box)
     fields = pl.pallas_call(
         functools.partial(kernel, nx, ny),
@@ -222,7 +245,7 @@
         in_specs=[hbm] * 11,
         out_specs=[vmem] * 3,
         scratch_shapes=[cell_int, cell_int, cell, cell] + [pltpu.SMEM(a.shape, a.dtype) for a in small]
-        + messages + messages + [pltpu.VMEM((2, wx, depth), jnp.float32)]
+        + sent + messages + [pltpu.VMEM((2, wx, depth), jnp.float32)]
         + [pltpu.SemaphoreType.DMA((11,)),
            pltpu.SemaphoreType.DMA((steps, 6)), pltpu.SemaphoreType.DMA((steps, 6))],
         compiler_params=pltpu.CompilerParams(

time: 19.2 us -> 19.2 us (level)
  no operation moved by 1% of the time
where the time goes in v3:
time: 19.2 us; the launch traced here: 19.1 us
  Pallas kernels  18.4 us (96%)
  between operations  0.64 us (3%)
    pallas_call x1, Pallas kernels, body(): pl.pallas_call(functools.partial(kernel, nx, ny), out_shape=[pltpu.VMEM(e...  17.4 us
    pallas_call x1, Pallas kernels, body(): pl.pallas_call(write_out, out_shape=[jax.ShapeDtypeStruct(e_field.shape,...  1.03 us

profile of v3, /device:TPU:0, one launch (start us, length us, event | category | flops | bytes accessed | tf_op | source)
XLA Modules:
  0.0 19.1 jit_solution(13901498104531119619)
XLA Ops:
  0.6 17.4 %shard_map.130 = (f32[3,16,8,256]{3,2,1,0:T(8,128)S(1)}, f32[3,16,8,256]{3,2,1,0:T(8,128)S(1)}, f32[3,16,8,256]{3,2,1,0:T(8,128)S(1)}) custom-call(f32[3,16,8,256]{3,2,1,0:T(8,128)} %e_in.1, f32[3,16,8,256]{3,2,1,0:T(8,128)} %h_in.1, f32[3,16,8,256]{3,2,1,0:T(8,128)} %j_in.1, s32[16,8,256]{2,1,0:T(8,128)} %mat_in.1, s32[16,8,256]{2,1,0:T(8,128)} %coat_in.1, ...), custom_call_target="tpu_custom_call" | custom-call | tf_op jit(solution)/shard_map/pallas_call | solution.py:242
  18.0 1.0 %shard_map.131 = (f32[3,16,8,256]{3,2,1,0:T(8,128)}, f32[3,16,8,256]{3,2,1,0:T(8,128)}, f32[3,16,8,256]{3,2,1,0:T(8,128)}) custom-call(f32[3,16,8,256]{3,2,1,0:T(8,128)S(1)} %get-tuple-element.6.refs_0_, f32[3,16,8,256]{3,2,1,0:T(8,128)S(1)} %get-tuple-element.7.refs_1_, f32[3,16,8,256]{3,2,1,0:T(8,128)S(1)} %get-tuple-element.8.refs_2_), custom_call_target="tpu_custom_call" | custom-call | tf_op jit(solution)/shard_map/pallas_call | solution.py:254
